TPU v7x, 128 devices: a whole 4x4x4 slice. The times are simulated.
128 devices in a mesh: wide: 16 (over z, x), narrow: 8 (over y, core).
Axes of the slice: x: 4, y: 4, z: 4, core: 2. Of those that a mesh axis runs over, the one named last changes fastest.
Arguments:
- cotangent: float32 [1536, 256, 256], P(('wide', 'narrow')), may hold values from -6 to 6
- row_basis: float32 [1536, 256, 128], P(('wide', 'narrow')), may hold values from -0.375 to 0.375
- col_basis: float32 [1536, 256, 128], P(('wide', 'narrow')), may hold values from -0.5 to 0.5
- leaf_up: float32 [1536, 128, 128], P(('wide', 'narrow')), may hold values from -0.15625 to 0.15625
- node_up: float32 [128, 128, 128], P(('wide', 'narrow')), may hold values from -0.1875 to 0.1875
- node_couple: float32 [128, 2, 128, 128], P(('wide', 'narrow')), may hold values from -0.375 to 0.375
- group_couple: float32 [16, 8, 128, 128], P('wide', 'narrow'), may hold values from -0.1875 to 0.1875
- node_down: float32 [128, 128, 128], P(('wide', 'narrow')), may hold values from -0.5 to 0.5
- leaf_down: float32 [1536, 128, 128], P(('wide', 'narrow')), may hold values from -0.5 to 0.5
- near_blocks: float32 [1536, 4, 256, 256], P(('wide', 'narrow')), may hold values from -0.1875 to 0.1875
- near_index: int32 [1536, 4], P(('wide', 'narrow')), may hold values from 0 to 1535, as said below
- far_nodes: int32 [128, 2], P(('wide', 'narrow')), may hold values from 0 to 7, as said below
- far_groups: int32 [16, 8], P('wide', 'narrow'), may hold values from 0 to 15, as said below
Outputs:
- product: float32 [1536, 256, 256], P(('wide', 'narrow'))
Inputs may be any that keep to these rules, and one draw needn't show every extreme that they name: near_index[l, 0] is l; every other entry differs from l by 1 to 2. far_nodes[d, j] never equals d % 8; the entries of a row differ. far_groups[g, j] never equals g; the entries of a row differ.
All inputs are finite; a program needn't handle non-finite values.
Results may differ from a plain program's by a relative error of at most 0.000062.
Values sent between devices are 32-bit elements; how exact they have to be, the bound alone decides.
A program may use at most 128 MiB of HBM per device.

v0:
```python
import jax
import jax.numpy as jnp
from jax import lax
from jax.sharding import PartitionSpec as P

NEAR_REACH = 2
HIGH = lax.Precision.HIGHEST


def from_behind(value, axis, steps):
    count = lax.axis_size(axis)
    leading, last = (max(0, -steps), min(count, count - steps))
    return lax.ppermute(value, axis, [(source, source + steps) for source in range(leading, last)])


def shards(
    cotangent,
    row_basis,
    col_basis,
    leaf_up,
    node_up,
    node_couple,
    group_couple,
    node_down,
    leaf_down,
    near_blocks,
    near_index,
    far_nodes,
    far_groups,
):
    leaves = cotangent.shape[0]
    lower = from_behind(cotangent[leaves - NEAR_REACH :], ("wide", "narrow"), 1)
    upper = from_behind(cotangent[:NEAR_REACH], ("wide", "narrow"), -1)
    leaf_coeffs = jnp.einsum("lpk,lpv->lkv", row_basis, cotangent, precision=HIGH)
    node_coeffs = jnp.einsum("lkm,lkv->mv", leaf_up, leaf_coeffs, precision=HIGH)
    up_term = jnp.dot(node_up[0].T, node_coeffs, precision=HIGH)
    siblings = lax.all_gather(node_coeffs[None], "narrow", axis=0, tiled=True)
    group_coeffs = lax.psum(up_term, "narrow")
    picked = siblings[far_nodes[0]]
    node_out = jnp.einsum("jkm,jkv->mv", node_couple[0], picked, precision=HIGH)
    all_groups = lax.all_gather(group_coeffs[None], "wide", axis=0, tiled=True)
    picked_groups = all_groups[far_groups[0]]
    partial_value = jnp.einsum("jkm,jkv->mv", group_couple[0], picked_groups, precision=HIGH)
    group_out = lax.psum(partial_value, "narrow")
    node_total = node_out + jnp.dot(node_down[0], group_out, precision=HIGH)
    leaf_total = jnp.einsum("lmk,kv->lmv", leaf_down, node_total, precision=HIGH)
    far_part = jnp.einsum("lpk,lkv->lpv", col_basis, leaf_total, precision=HIGH)
    extended = jnp.concatenate([lower, cotangent, upper], axis=0)
    node_rank = lax.axis_index("wide") * lax.axis_size("narrow") + lax.axis_index("narrow")
    first_leaf = node_rank * leaves - NEAR_REACH
    local_index = near_index - first_leaf
    sources = extended[local_index]
    near_part = jnp.einsum("ljpq,ljpv->lqv", near_blocks, sources, precision=HIGH)
    return far_part + near_part


def solution(mesh):
    in_specs = (
        P(("wide", "narrow"), None, None),
        P(("wide", "narrow"), None, None),
        P(("wide", "narrow"), None, None),
        P(("wide", "narrow"), None, None),
        P(("wide", "narrow"), None, None),
        P(("wide", "narrow"), None, None, None),
        P("wide", "narrow", None, None),
        P(("wide", "narrow"), None, None),
        P(("wide", "narrow"), None, None),
        P(("wide", "narrow"), None, None, None),
        P(("wide", "narrow"), None),
        P(("wide", "narrow"), None),
        P("wide", "narrow"),
    )
    out_specs = P(("wide", "narrow"), None, None)
    return jax.shard_map(shards, mesh=mesh, in_specs=in_specs, out_specs=out_specs, check_vma=False)
```

profile of v0, /device:TPU:0, one launch (start us, length us, event | category | flops | bytes accessed | tf_op | source)
XLA Modules:
  0.0 259.9 jit_solution(13110974289088481287)
XLA Ops:
  6.5 0.0 copy-start
  6.5 0.0 copy-start.2
  6.5 0.0 copy-start.4
  6.5 0.0 all-reduce.3.cloned.1.call-start
  6.5 7.7 %fusion.14 = f32[12,128,256]{1,2,0:T(8,128)S(1)} fusion(f32[12,256,128]{2,1,0:T(8,128)} %param.14, f32[12,256,256]{2,1,0:T(8,128)} %param.13), kind=kOutput, calls=%fused_computation.26 | convolution fusion | flops 1207959552 | bytes 6291456 | tf_op jit(solution)/shard_map/lpk,lpv->lkv/dot_general | solution.py:34
  14.3 0.0 copy-done.2
  14.3 0.0 copy-start.7
  14.3 0.0 copy-start.8
  14.3 1.4 fusion.15
  15.7 0.0 copy-done.4
  15.7 0.0 copy-start.1
  15.7 0.9 convolution_bitcast_fusion.2
  16.6 0.0 all-reduce.3.cloned.1.call-update
  16.7 0.0 all-gather.6.cloned.1.call-start
  16.7 0.0 copy-done.1
  16.7 0.7 all-gather.6.cloned.1.call-update
  17.4 0.0 all-gather.4.cloned.1.call-start
  17.5 61.0 %all-reduce.3.cloned.1.call-done = f32[1,128,256]{1,2,0:T(8,128)} async-done(((f32[1,128,256]{1,2,0:T(8,128)}), f32[1,128,256]{1,2,0:T(8,128)}) %all-reduce.3.cloned.1.call-update) | async-done | bytes 131088 | tf_op jit(solution)/shard_map/psum | solution.py:38
  78.5 1.7 copy.25
  80.2 0.0 all-gather.4.cloned.1.call-update
  80.2 0.0 all-reduce.5.cloned.1.call-start
  80.2 2.1 fusion.13
  82.3 1.3 collective-permute-start
  83.7 1.5 collective-permute-start.1
  85.1 0.0 copy-done.7
  85.8 0.1 copy.26
  85.9 0.1 reshape.69
  86.0 0.0 copy-done.8
  86.0 0.0 collective-permute-done
  86.1 1.4 collective-permute-done.1
  87.5 4.3 %pad_maximum_fusion = f32[16,256,256]{2,1,0:T(8,128)} fusion(f32[2,256,256]{2,1,0:T(8,128)S(1)} %collective-permute-done.1, f32[12,256,256]{2,1,0:T(8,128)} %param.13, f32[2,256,256]{2,1,0:T(8,128)S(1)} %collective-permute-done), kind=kLoop, calls=%fused_computation.2 | loop fusion | flops 2097152 | bytes 8388608 | tf_op jit(solution)/shard_map/concatenate | solution.py:48
  91.7 0.0 copy-start.5
  91.7 10.0 %gather_fusion.1 = f32[48,256,256]{2,1,0:T(8,128)} fusion(f32[16,256,256]{2,1,0:T(8,128)} %pad_maximum_fusion, s32[1024]{0:T(1024)S(1)} %pad_clamp_fusion), kind=kCustom, calls=%fused_computation.1 | custom fusion | bytes 25166016 | tf_op jit(solution)/shard_map/gather | solution.py:52
  101.8 0.0 copy-start.3
  101.8 0.0 copy-start.6
  101.8 5.8 %all-gather.6.cloned.1.call-done = f32[1024,256]{0,1:T(8,128)} async-done(((f32[128,256]{0,1:T(8,128)}), f32[1024,256]{0,1:T(8,128)}) %all-gather.6.cloned.1.call-update) | async-done | bytes 1048592 | tf_op jit(solution)/shard_map/all_gather | solution.py:37
  107.6 1.6 copy.34
  109.2 0.6 gather_fusion
  109.7 45.5 %all-gather.4.cloned.1.call-done = f32[16,128,256]{2,1,0:T(8,128)} async-done(((f32[1,128,256]{2,1,0:T(8,128)}), f32[16,128,256]{2,1,0:T(8,128)}) %all-gather.4.cloned.1.call-update) | async-done | bytes 2097168 | tf_op jit(solution)/shard_map/all_gather | solution.py:41
  155.2 0.0 copy-done.5
  155.2 1.9 convolution_bitcast_fusion.1
  157.2 0.0 all-reduce.5.cloned.1.call-update
  157.2 0.0 copy-done.3
  157.2 0.6 convolution_bitcast_fusion
  157.8 58.3 %all-reduce.5.cloned.1.call-done = f32[128,256]{0,1:T(8,128)} async-done(((f32[128,256]{0,1:T(8,128)}), f32[128,256]{0,1:T(8,128)}) %all-reduce.5.cloned.1.call-update) | async-done | bytes 131088 | tf_op jit(solution)/shard_map/psum | solution.py:44
  216.1 0.0 copy-done.6
  216.1 1.2 fusion.3
  217.3 2.5 fusion.16
  219.9 0.0 copy-done
  219.9 2.9 %fusion.1 = f32[12,256,256]{2,1,0:T(8,128)S(1)} fusion(f32[12,256,128]{2,1,0:T(8,128)S(1)} %copy-done, f32[256,12,128]{2,0,1:T(8,128)S(1)} %fusion.16), kind=kOutput, calls=%fused_computation.5 | convolution fusion | flops 1207959552 | bytes 6291456 | tf_op jit(solution)/shard_map/lpk,lkv->lpv/dot_general | solution.py:47
  222.8 27.0 %fusion = f32[12,256,256]{1,2,0:T(8,128)} fusion(f32[12,256,256]{2,1,0:T(8,128)S(1)} %fusion.1, f32[12,4,256,256]{3,2,1,0:T(8,128)} %bitcast.62, f32[12,4,256,256]{3,2,1,0:T(8,128)} %param.22), kind=kOutput, calls=%fused_computation.4 | convolution fusion | flops 9664462848 | bytes 31457280 | tf_op jit(solution)/shard_map/ljpq,ljpv->lqv/dot_general | solution.py:53
  249.8 3.5 %copy.28 = f32[12,256,256]{2,1,0:T(8,128)} copy(f32[12,256,256]{1,2,0:T(8,128)} %fusion) | data formatting | bytes 6291456 | tf_op jit(solution)/shard_map/add | solution.py:54
  (4 shorter events, 0.0 us)
Async XLA Ops:
  6.5 213.3 %copy-start = (f32[12,256,128]{2,1,0:T(8,128)S(1)}, f32[12,256,128]{2,1,0:T(8,128)}, u32[]{:S(2)}) copy-start(f32[12,256,128]{2,1,0:T(8,128)} %param.15) | copy-start | bytes 4718596
  6.5 7.7 %copy-start.2 = (f32[12,128,128]{2,1,0:T(8,128)S(1)}, f32[12,128,128]{2,1,0:T(8,128)}, u32[]{:S(2)}) copy-start(f32[12,128,128]{2,1,0:T(8,128)} %param.16) | copy-start | bytes 2359300
  6.5 9.2 %copy-start.4 = (f32[1,128,128]{2,1,0:T(8,128)S(1)}, f32[1,128,128]{2,1,0:T(8,128)}, u32[]{:S(2)}) copy-start(f32[1,128,128]{2,1,0:T(8,128)} %param.17) | copy-start | bytes 196612
  6.5 72.0 %all-reduce.3.cloned.1.call-start = ((), (), s32[]{:S(2)}) async-start(), calls=%async_computation | async-start | bytes 262144 | tf_op jit(solution)/shard_map/psum | solution.py:38
  14.3 70.9 %copy-start.7 = (s32[12,4]{0,1:T(4,128)S(1)}, s32[12,4]{0,1:T(4,128)}, u32[]{:S(2)}) copy-start(s32[12,4]{0,1:T(4,128)} %param.23) | copy-start | bytes 580
  14.3 71.7 %copy-start.8 = (s32[1,2]{1,0:T(1,128)S(1)}, s32[1,2]{1,0:T(1,128)}, u32[]{:S(2)}) copy-start(s32[1,2]{1,0:T(1,128)} %param.24) | copy-start | bytes 28
  15.7 1.0 copy-start.1
  16.7 90.9 %all-gather.6.cloned.1.call-start = ((), (), s32[]{:S(2)}) async-start(), calls=%async_computation.3 | async-start | bytes 1179648 | tf_op jit(solution)/shard_map/all_gather | solution.py:37
  17.4 137.8 %all-gather.4.cloned.1.call-start = ((), (), s32[]{:S(2)}) async-start(), calls=%async_computation.1 | async-start | bytes 2228224 | tf_op jit(solution)/shard_map/all_gather | solution.py:41
  80.2 135.9 %all-reduce.5.cloned.1.call-start = ((), (), s32[]{:S(2)}) async-start(), calls=%async_computation.2 | async-start | bytes 262144 | tf_op jit(solution)/shard_map/psum | solution.py:44
  82.3 3.7 %collective-permute-start = (f32[2,256,256]{2,1,0:T(8,128)}, f32[2,256,256]{2,1,0:T(8,128)S(1)}, u32[]{:S(2)}, u32[]{:S(2)}) collective-permute-start(f32[2,256,256]{2,1,0:T(8,128)} %get-tuple-element.16), channel_id=1, source_target_pairs={{0,1},{1,2},{2,3},{3,4},{4,5},{5,6},{6,7},{7,8},{8,9},{9,10},{10,1... | collective-permute-start | bytes 1572872 | tf_op jit(solution)/shard_map/ppermute | solution.py:13
  83.7 3.8 %collective-permute-start.1 = (f32[2,256,256]{2,1,0:T(8,128)S(1)}, f32[2,256,256]{2,1,0:T(8,128)S(1)}, u32[]{:S(2)}, u32[]{:S(2)}) collective-permute-start(f32[2,256,256]{2,1,0:T(8,128)S(1)} %get-tuple-element.17), channel_id=1, source_target_pairs={{1,0},{2,1},{3,2},{4,3},{5,4},{6,5},{7,6},{8,7},{9,8},{10,9},{11,1... | collective-permute-start | bytes 1572872 | tf_op jit(solution)/shard_map/ppermute | solution.py:13
  91.7 63.5 %copy-start.5 = (f32[1,1,128,128]{3,2,1,0:T(8,128)S(1)}, f32[1,1,128,128]{3,2,1,0:T(8,128)}, u32[]{:S(2)}) copy-start(f32[1,1,128,128]{3,2,1,0:T(8,128)} %param.19) | copy-start | bytes 196612
  101.8 55.5 %copy-start.3 = (f32[1,2,128,128]{3,2,1,0:T(8,128)S(1)}, f32[1,2,128,128]{3,2,1,0:T(8,128)}, u32[]{:S(2)}) copy-start(f32[1,2,128,128]{3,2,1,0:T(8,128)} %param.18) | copy-start | bytes 393220
  101.8 114.4 %copy-start.6 = (f32[1,128,128]{2,1,0:T(8,128)S(1)}, f32[1,128,128]{2,1,0:T(8,128)}, u32[]{:S(2)}) copy-start(f32[1,128,128]{2,1,0:T(8,128)} %param.20) | copy-start | bytes 196612
Sparse Core Ops, SparseCore 0:
  16.8 61.6 all-reduce.2
  80.3 27.2 all-gather.5
  110.0 45.2 all-gather.3
  157.5 58.5 all-reduce.4
where the time goes:
time: 260 us
  waiting for transfers between devices  173 us (67%)
  matrix products  46.2 us (18%)
  local copies, waits for them, and re-layouts  19.7 us (8%)
  between operations  14 us (5%)
  other arithmetic  4.28 us (2%)
  starting transfers between devices  2.91 us (1%)
    psum x1, waiting for transfers between devices, shards(): group_coeffs = lax.psum(up_term, 'narrow')  61 us
    psum x1, waiting for transfers between devices, shards(): group_out = lax.psum(partial_value, 'narrow')  58.3 us
    all_gather x1, waiting for transfers between devices, shards(): all_groups = lax.all_gather(group_coeffs[None], 'wide', axis=0, tiled=True)  45.5 us
    dot_general x1, matrix products, shards(): jnp.einsum('ljpq,ljpv->lqv', near_blocks, sources, precision=HIGH)  27 us
    gather x1, local copies, waits for them, and re-layouts, shards(): sources = extended[local_index]  10 us
    dot_general x1, matrix products, shards(): jnp.einsum('lpk,lpv->lkv', row_basis, cotangent, precision=HIGH)  7.71 us
    all_gather x1, waiting for transfers between devices, shards(): siblings = lax.all_gather(node_coeffs[None], 'narrow', axis=0, tiled=True)  5.84 us
  transfers between devices with their start and end apart: 6, of which 5 were waited for; matrix products, arithmetic and copies ran while one was open for 8% of the time, Pallas kernels for 0%

commit v1 on v0

--- a/solution.py
+++ b/solution.py
@@ -35,7 +35,11 @@
     node_coeffs = jnp.einsum("lkm,lkv->mv", leaf_up, leaf_coeffs, precision=HIGH)
     up_term = jnp.dot(node_up[0].T, node_coeffs, precision=HIGH)
     siblings = lax.all_gather(node_coeffs[None], "narrow", axis=0, tiled=True)
-    group_coeffs = lax.psum(up_term, "narrow")
+    group_coeffs = up_term
+    for hop in (1, 2, 4):
+        group_coeffs = group_coeffs + lax.ppermute(
+            group_coeffs, "narrow", [(dev, dev ^ hop) for dev in range(8)]
+        )
     picked = siblings[far_nodes[0]]
     node_out = jnp.einsum("jkm,jkv->mv", node_couple[0], picked, precision=HIGH)
     all_groups = lax.all_gather(group_coeffs[None], "wide", axis=0, tiled=True)

time: 260 us -> 198 us (0.76)
  waiting for transfers between devices: 173 us -> 106 us
  starting transfers between devices: 2.91 us -> 8.04 us
    psum x1 -> x0, waiting for transfers between devices: 61 us -> none  [shards(): group_coeffs = lax.psum(up_term, 'narrow')]
    all_gather x1, waiting for transfers between devices: 45.5 us -> 36 us  [shards(): all_groups = lax.all_gather(group_coeffs[None], 'wide', axis=0, tiled=True)]
    ppermute x0 -> x3, waiting for transfers between devices: none -> 8.87 us  [shards(): lax.ppermute(group_coeffs, 'narrow', [(dev, dev ^ hop) for dev in range(8)])]
    all_gather x1, waiting for transfers between devices: 5.84 us -> 0.01 us  [shards(): siblings = lax.all_gather(node_coeffs[None], 'narrow', axis=0, tiled=True)]
    ppermute x0 -> x3, starting transfers between devices: none -> 5.18 us  [shards(): lax.ppermute(group_coeffs, 'narrow', [(dev, dev ^ hop) for dev in range(8)])]
  transfers between devices with their start and end apart: 6 -> 8, of which waited for: 5 -> 6; matrix products, arithmetic and copies ran while one was open for 8% -> 11% of each run, Pallas kernels for 0% -> 0%
where the time goes in v1:
time: 198 us
  waiting for transfers between devices  106 us (54%)
  matrix products  44.9 us (23%)
  local copies, waits for them, and re-layouts  20 us (10%)
  between operations  14 us (7%)
  starting transfers between devices  8.04 us (4%)
  other arithmetic  4.91 us (2%)
    psum x1, waiting for transfers between devices, shards(): group_out = lax.psum(partial_value, 'narrow')  58 us
    all_gather x1, waiting for transfers between devices, shards(): all_groups = lax.all_gather(group_coeffs[None], 'wide', axis=0, tiled=True)  36 us
    dot_general x1, matrix products, shards(): jnp.einsum('ljpq,ljpv->lqv', near_blocks, sources, precision=HIGH)  27 us
    gather x1, local copies, waits for them, and re-layouts, shards(): sources = extended[local_index]  9.9 us
    ppermute x3, waiting for transfers between devices, shards(): lax.ppermute(group_coeffs, 'narrow', [(dev, dev ^ hop) for dev in range(8)])  8.87 us
    dot_general x1, matrix products, shards(): jnp.einsum('lpk,lpv->lkv', row_basis, cotangent, precision=HIGH)  7.71 us
    ppermute x3, starting transfers between devices, shards(): lax.ppermute(group_coeffs, 'narrow', [(dev, dev ^ hop) for dev in range(8)])  5.18 us
    concatenate x1, other arithmetic, shards(): extended = jnp.concatenate([lower, cotangent, upper], axis=0)  4.2 us
  transfers between devices with their start and end apart: 8, of which 6 were waited for; matrix products, arithmetic and copies ran while one was open for 11% of the time, Pallas kernels for 0%

profile of v1, /device:TPU:0, one launch (start us, length us, event | category | flops | bytes accessed | tf_op | source)
XLA Modules:
  0.0 197.7 jit_solution(12663110009314069732)
XLA Ops:
  6.5 0.0 copy-start
  6.5 0.0 copy-start.1
  6.5 0.0 copy-start.4
  6.5 0.0 all-gather.5.cloned.1.call-start
  6.5 7.7 %fusion.11 = f32[12,128,256]{1,2,0:T(8,128)S(1)} fusion(f32[12,256,128]{2,1,0:T(8,128)} %param.14, f32[12,256,256]{2,1,0:T(8,128)} %param.13), kind=kOutput, calls=%fused_computation.24 | convolution fusion | flops 1207959552 | bytes 6291456 | tf_op jit(solution)/shard_map/lpk,lpv->lkv/dot_general | solution.py:34
  14.3 0.0 copy-done.1
  14.3 0.0 copy-start.7
  14.3 0.0 copy-start.8
  14.3 2.1 %fusion.12 = f32[256,128,1]{1,0,2:T(8,128)} fusion(f32[12,128,256]{1,2,0:T(8,128)S(1)} %fusion.11, f32[12,128,128]{2,1,0:T(8,128)S(1)} %copy-done.1), kind=kOutput, calls=%fused_computation.25 | convolution fusion | flops 603979776 | bytes 2490368 | tf_op jit(solution)/shard_map/lkm,lkv->mv/dot_general | solution.py:35
  16.3 0.0 all-gather.5.cloned.1.call-update
  16.4 0.0 all-gather.7.cloned.1.call-start
  16.4 0.0 copy-done.4
  16.4 1.2 convolution_bitcast_fusion.2
  17.6 0.1 collective-permute-start
  17.7 1.3 collective-permute-done
  19.0 1.7 collective-permute-start.1
  20.8 3.9 %collective-permute-done.1 = f32[128,256]{0,1:T(8,128)S(1)} collective-permute-done((f32[128,256]{0,1:T(8,128)S(1)}, f32[128,256]{0,1:T(8,128)S(1)}, u32[]{:S(2)}, u32[]{:S(2)}) %collective-permute-start.1) | collective-permute-done | bytes 131104 | tf_op jit(solution)/shard_map/ppermute | solution.py:40
  24.7 3.4 %collective-permute-start.2 = (f32[128,256]{0,1:T(8,128)S(1)}, f32[128,256]{0,1:T(8,128)S(1)}, u32[]{:S(2)}, u32[]{:S(2)}) collective-permute-start(f32[128,256]{0,1:T(8,128)S(1)} %add.46), channel_id=1, source_target_pairs={{0,4},{1,5},{2,6},{3,7},{4,0},{5,1},{6,2},{7,3},{8,12},{9,13},{10,... | collective-permute-start | bytes 393224 | tf_op jit(solution)/shard_map/ppermute | solution.py:40
  28.0 3.6 %collective-permute-done.2 = f32[128,256]{0,1:T(8,128)S(1)} collective-permute-done((f32[128,256]{0,1:T(8,128)S(1)}, f32[128,256]{0,1:T(8,128)S(1)}, u32[]{:S(2)}, u32[]{:S(2)}) %collective-permute-start.2) | collective-permute-done | bytes 131104 | tf_op jit(solution)/shard_map/ppermute | solution.py:40
  31.7 0.7 add.47
  32.4 0.0 all-gather.7.cloned.1.call-update
  32.4 0.0 all-reduce.2.cloned.1.call-start
  32.4 2.1 %fusion.10 = (f32[2,256,256]{2,1,0:T(8,128)}, f32[2,256,256]{2,1,0:T(8,128)S(1)}) fusion(f32[12,256,256]{2,1,0:T(8,128)} %param.13), kind=kLoop, calls=%fused_computation.23 | loop fusion | bytes 2097152 | tf_op jit(solution)/shard_map/slice | solution.py:32
  34.5 1.3 collective-permute-start.3
  35.8 1.5 collective-permute-start.4
  37.3 0.0 copy-done.7
  38.0 0.1 copy.18
  38.1 0.1 reshape.69
  38.2 0.0 copy-done.8
  38.2 0.0 collective-permute-done.3
  38.2 2.9 %collective-permute-done.4 = f32[2,256,256]{2,1,0:T(8,128)S(1)} collective-permute-done((f32[2,256,256]{2,1,0:T(8,128)S(1)}, f32[2,256,256]{2,1,0:T(8,128)S(1)}, u32[]{:S(2)}, u32[]{:S(2)}) %collective-permute-start.4) | collective-permute-done | bytes 524320 | tf_op jit(solution)/shard_map/ppermute | solution.py:13
  41.1 4.2 %pad_maximum_fusion = f32[16,256,256]{2,1,0:T(8,128)} fusion(f32[2,256,256]{2,1,0:T(8,128)S(1)} %collective-permute-done.4, f32[12,256,256]{2,1,0:T(8,128)} %param.13, f32[2,256,256]{2,1,0:T(8,128)S(1)} %collective-permute-done.3), kind=kLoop, calls=%fused_computation.2 | loop fusion | flops 2097152 | bytes 8388608 | tf_op jit(solution)/shard_map/concatenate | solution.py:52
  45.3 9.9 %gather_fusion.1 = f32[48,256,256]{2,1,0:T(8,128)} fusion(f32[16,256,256]{2,1,0:T(8,128)} %pad_maximum_fusion, s32[1024]{0:T(1024)S(1)} %pad_clamp_fusion), kind=kCustom, calls=%fused_computation.1 | custom fusion | bytes 25166016 | tf_op jit(solution)/shard_map/gather | solution.py:56
  55.2 0.0 copy-start.5
  55.2 0.0 all-gather.5.cloned.1.call-done
  55.2 1.6 copy.23
  56.8 0.0 copy-start.3
  56.8 0.0 copy-start.6
  56.8 0.6 gather_fusion
  57.4 0.0 copy-start.2
  57.4 36.0 %all-gather.7.cloned.1.call-done = f32[2048,256]{0,1:T(8,128)} async-done(((f32[128,256]{0,1:T(8,128)}), f32[2048,256]{0,1:T(8,128)}) %all-gather.7.cloned.1.call-update) | async-done | bytes 2097168 | tf_op jit(solution)/shard_map/all_gather | solution.py:45
  93.4 2.0 copy.24
  95.4 0.1 constant_dynamic-slice_fusion
  95.5 0.0 copy-done.5
  95.5 0.9 convolution_bitcast_fusion.1
  96.4 0.0 all-reduce.2.cloned.1.call-update
  96.4 0.0 copy-done.3
  96.4 0.6 convolution_bitcast_fusion
  97.0 58.0 %all-reduce.2.cloned.1.call-done = f32[128,256]{0,1:T(8,128)} async-done(((f32[128,256]{0,1:T(8,128)}), f32[128,256]{0,1:T(8,128)}) %all-reduce.2.cloned.1.call-update) | async-done | bytes 131088 | tf_op jit(solution)/shard_map/psum | solution.py:48
  155.1 0.0 copy-done.6
  155.1 1.2 fusion.3
  156.3 0.0 copy-done.2
  156.3 1.4 fusion.13
  157.7 0.0 copy-done
  157.7 2.9 %fusion.1 = f32[12,256,256]{2,1,0:T(8,128)S(1)} fusion(f32[12,256,128]{2,1,0:T(8,128)S(1)} %copy-done, f32[256,12,128]{2,0,1:T(8,128)S(1)} %fusion.13), kind=kOutput, calls=%fused_computation.5 | convolution fusion | flops 1207959552 | bytes 6291456 | tf_op jit(solution)/shard_map/lpk,lkv->lpv/dot_general | solution.py:51
  160.6 27.0 %fusion = f32[12,256,256]{1,2,0:T(8,128)} fusion(f32[12,256,256]{2,1,0:T(8,128)S(1)} %fusion.1, f32[12,4,256,256]{3,2,1,0:T(8,128)} %bitcast.63, f32[12,4,256,256]{3,2,1,0:T(8,128)} %param.22), kind=kOutput, calls=%fused_computation.4 | convolution fusion | flops 9664462848 | bytes 31457280 | tf_op jit(solution)/shard_map/ljpq,ljpv->lqv/dot_general | solution.py:57
  187.6 3.5 %copy.20 = f32[12,256,256]{2,1,0:T(8,128)} copy(f32[12,256,256]{1,2,0:T(8,128)} %fusion) | data formatting | bytes 6291456 | tf_op jit(solution)/shard_map/add | solution.py:58
  (6 shorter events, 0.1 us)
Async XLA Ops:
  6.5 151.1 %copy-start = (f32[12,256,128]{2,1,0:T(8,128)S(1)}, f32[12,256,128]{2,1,0:T(8,128)}, u32[]{:S(2)}) copy-start(f32[12,256,128]{2,1,0:T(8,128)} %param.15) | copy-start | bytes 4718596
  6.5 7.7 %copy-start.1 = (f32[12,128,128]{2,1,0:T(8,128)S(1)}, f32[12,128,128]{2,1,0:T(8,128)}, u32[]{:S(2)}) copy-start(f32[12,128,128]{2,1,0:T(8,128)} %param.16) | copy-start | bytes 2359300
  6.5 9.9 %copy-start.4 = (f32[1,128,128]{2,1,0:T(8,128)S(1)}, f32[1,128,128]{2,1,0:T(8,128)}, u32[]{:S(2)}) copy-start(f32[1,128,128]{2,1,0:T(8,128)} %param.17) | copy-start | bytes 196612
  6.5 48.7 %all-gather.5.cloned.1.call-start = ((), (), s32[]{:S(2)}) async-start(), calls=%async_computation.1 | async-start | bytes 1179648 | tf_op jit(solution)/shard_map/all_gather | solution.py:37
  14.3 23.1 %copy-start.7 = (s32[12,4]{0,1:T(4,128)S(1)}, s32[12,4]{0,1:T(4,128)}, u32[]{:S(2)}) copy-start(s32[12,4]{0,1:T(4,128)} %param.23) | copy-start | bytes 580
  14.3 23.9 %copy-start.8 = (s32[1,2]{1,0:T(1,128)S(1)}, s32[1,2]{1,0:T(1,128)}, u32[]{:S(2)}) copy-start(s32[1,2]{1,0:T(1,128)} %param.24) | copy-start | bytes 28
  16.4 77.0 %all-gather.7.cloned.1.call-start = ((), (), s32[]{:S(2)}) async-start(), calls=%async_computation.2 | async-start | bytes 2228224 | tf_op jit(solution)/shard_map/all_gather | solution.py:45
  17.6 1.4 collective-permute-start
  19.0 5.6 %collective-permute-start.1 = (f32[128,256]{0,1:T(8,128)S(1)}, f32[128,256]{0,1:T(8,128)S(1)}, u32[]{:S(2)}, u32[]{:S(2)}) collective-permute-start(f32[128,256]{0,1:T(8,128)S(1)} %add.45), channel_id=1, source_target_pairs={{0,2},{1,3},{2,0},{3,1},{4,6},{5,7},{6,4},{7,5},{8,10},{9,11},{10,... | collective-permute-start | bytes 393224 | tf_op jit(solution)/shard_map/ppermute | solution.py:40
  24.7 7.0 %collective-permute-start.2 = (f32[128,256]{0,1:T(8,128)S(1)}, f32[128,256]{0,1:T(8,128)S(1)}, u32[]{:S(2)}, u32[]{:S(2)}) collective-permute-start(f32[128,256]{0,1:T(8,128)S(1)} %add.46), channel_id=1, source_target_pairs={{0,4},{1,5},{2,6},{3,7},{4,0},{5,1},{6,2},{7,3},{8,12},{9,13},{10,... | collective-permute-start | bytes 393224 | tf_op jit(solution)/shard_map/ppermute | solution.py:40
  32.4 122.7 %all-reduce.2.cloned.1.call-start = ((), (), s32[]{:S(2)}) async-start(), calls=%async_computation | async-start | bytes 262144 | tf_op jit(solution)/shard_map/psum | solution.py:48
  34.5 3.7 %collective-permute-start.3 = (f32[2,256,256]{2,1,0:T(8,128)}, f32[2,256,256]{2,1,0:T(8,128)S(1)}, u32[]{:S(2)}, u32[]{:S(2)}) collective-permute-start(f32[2,256,256]{2,1,0:T(8,128)} %get-tuple-element.16), channel_id=1, source_target_pairs={{0,1},{1,2},{2,3},{3,4},{4,5},{5,6},{6,7},{7,8},{8,9},{9,10},{10,1... | collective-permute-start | bytes 1572872 | tf_op jit(solution)/shard_map/ppermute | solution.py:13
  35.8 5.3 %collective-permute-start.4 = (f32[2,256,256]{2,1,0:T(8,128)S(1)}, f32[2,256,256]{2,1,0:T(8,128)S(1)}, u32[]{:S(2)}, u32[]{:S(2)}) collective-permute-start(f32[2,256,256]{2,1,0:T(8,128)S(1)} %get-tuple-element.17), channel_id=1, source_target_pairs={{1,0},{2,1},{3,2},{4,3},{5,4},{6,5},{7,6},{8,7},{9,8},{10,9},{11,1... | collective-permute-start | bytes 1572872 | tf_op jit(solution)/shard_map/ppermute | solution.py:13
  55.2 40.3 %copy-start.5 = (f32[1,1,128,128]{3,2,1,0:T(8,128)S(1)}, f32[1,1,128,128]{3,2,1,0:T(8,128)}, u32[]{:S(2)}) copy-start(f32[1,1,128,128]{3,2,1,0:T(8,128)} %param.19) | copy-start | bytes 196612
  56.8 39.6 %copy-start.3 = (f32[1,2,128,128]{3,2,1,0:T(8,128)S(1)}, f32[1,2,128,128]{3,2,1,0:T(8,128)}, u32[]{:S(2)}) copy-start(f32[1,2,128,128]{3,2,1,0:T(8,128)} %param.18) | copy-start | bytes 393220
  56.8 98.2 %copy-start.6 = (f32[1,128,128]{2,1,0:T(8,128)S(1)}, f32[1,128,128]{2,1,0:T(8,128)}, u32[]{:S(2)}) copy-start(f32[1,128,128]{2,1,0:T(8,128)} %param.20) | copy-start | bytes 196612
  57.4 98.9 %copy-start.2 = (f32[12,128,128]{2,1,0:T(8,128)S(1)}, f32[12,128,128]{2,1,0:T(8,128)}, u32[]{:S(2)}) copy-start(f32[12,128,128]{2,1,0:T(8,128)} %param.21) | copy-start | bytes 2359300
Sparse Core Ops, SparseCore 0:
  16.5 27.1 all-gather.4
  45.8 47.5 all-gather.6
  96.5 58.4 all-reduce.1
